TPU v7x, 128 devices: a whole 4x4x4 slice. The times are simulated.
128 devices in a mesh: row: 8 (over z, core), col: 16 (over y, x).
Axes of the slice: x: 4, y: 4, z: 4, core: 2. Of those that a mesh axis runs over, the one named last changes fastest.
Arguments:
- diag_tile: float32 [512, 512], P(('row', 'col')), may hold values from -1 to 2
- pivot_order: int32 [512], replicated, may hold values from 0 to 511, as said below
- panel_col: bfloat16 [64, 512, 512], P('row', 'col'), may hold values from -0.25 to 0.25
- panel_row: bfloat16 [64, 2, 64, 512], P('col', None, None, 'row'), may hold values from -5 to 5
- trail_factors: bfloat16 [64, 64, 2, 64, 512], P('row', 'col'), may hold values from -5 to 5
- tile_ranks: int32 [64, 64], P('row', 'col'), may hold values from 1 to 64
- pattern: int32 [64], P('col'), may hold values 0 or 1
- near_vals: bfloat16 [32768, 512], P(('row', 'col')), may hold values from -0.75 to 0.75
- near_dest: int32 [32768, 1], P(('row', 'col')), may hold values from 0 to 127; in each aligned block of 256 rows (0 to 255, 256 to 511, ...) at most 4 rows name the same one
- near_row: int32 [32768], P(('row', 'col')), may hold values from 0 to 255
- near_count: int32 [128], P(('row', 'col')), may hold values from 1 to 256, 16384 in all
Outputs:
- updated: bfloat16 [64, 64, 512, 512], P('row', 'col')
Inputs may be any that keep to these rules, and one draw needn't show every extreme that they name: `pivot_order`: a permutation of 0 to 511. `near_dest`: among the 256 slots of one device no device is named more than 4 times, and some device exactly 4 times. `near_count`: some partition has all 256 slots live.
All inputs are finite; a program needn't handle non-finite values. No bound on the sum of `pattern` or of `near_count` on one device may be relied on, other than what follows from the above.
Results may differ from a plain program's by a relative error of at most 0.0055.
Values may be sent and summed in bfloat16 or wider, within the bound.
A program may use at most 128 MiB of HBM per device.

v0:
```python
import jax
import jax.numpy as jnp
from jax import lax
from jax.sharding import PartitionSpec as P

B = 512
K = 64
TR = 8
TC = 4
NEAR = 256


highest_precision = lax.Precision.HIGHEST


def approximate_inverse(pivot_block):
    inverse = jnp.diag(1.0 / jnp.diagonal(pivot_block))
    for repeat in range(2):
        inner = jnp.dot(pivot_block, inverse, precision=highest_precision)
        inverse = 2.0 * inverse - jnp.dot(inverse, inner, precision=highest_precision)
    return inverse


def per_device(
    diag_tile,
    pivot_order,
    panel_col,
    panel_row,
    trail_factors,
    tile_ranks,
    pattern,
    near_vals,
    near_dest,
    near_row,
    near_count,
):
    n_rowdev = lax.axis_size("row")
    n_coldev = lax.axis_size("col")
    n_devices = n_rowdev * n_coldev
    capacity = 2 * NEAR // n_devices
    row_block = B // n_coldev
    panel_rows = TR * row_block
    slot_ids = jnp.arange(NEAR, dtype=jnp.int32)
    is_live = slot_ids < near_count[0]
    target_dev = near_dest[:, 0]
    earlier = (
        (target_dev[:, None] == target_dev[None, :])
        & is_live[None, :]
        & (slot_ids[None, :] < slot_ids[:, None])
    )
    position = jnp.sum(earlier.astype(jnp.int32), axis=1)
    target_slot = target_dev * capacity + position
    buffer_ids = jnp.arange(n_devices * capacity, dtype=jnp.int32)
    placing = (buffer_ids[:, None] == target_slot[None, :]) & is_live[None, :]
    send_vals = jnp.dot(
        placing.astype(jnp.bfloat16), near_vals, preferred_element_type=jnp.float32
    ).astype(jnp.bfloat16)
    index_pair = jnp.stack([near_row // 64 + 1, near_row % 64], axis=1).astype(jnp.float32)
    send_index = jnp.dot(
        placing.astype(jnp.float32), index_pair, precision=highest_precision
    ).astype(jnp.bfloat16)
    flat_vals = send_vals.reshape(n_devices, capacity, B)
    flat_index = send_index.reshape(n_devices, capacity, 2)
    recv_vals, recv_index = (
        lax.all_to_all(flat_vals, ("row", "col"), split_axis=0, concat_axis=0, tiled=True),
        lax.all_to_all(flat_index, ("row", "col"), split_axis=0, concat_axis=0, tiled=True),
    )
    recv_vals = recv_vals.reshape(n_devices * capacity, B)
    recv_index = recv_index.reshape(n_devices * capacity, 2).astype(jnp.float32)
    high_part = recv_index[:, 0] - 1.0
    local_row = (high_part * 64.0 + recv_index[:, 1]).astype(jnp.int32)
    arrived = high_part >= 0.0
    panel_ids = jnp.arange(panel_rows, dtype=jnp.int32)
    landing = (panel_ids[:, None] == local_row[None, :]) & arrived[None, :]
    additions = jnp.dot(landing.astype(jnp.bfloat16), recv_vals, preferred_element_type=jnp.float32)
    corrected = (panel_col.reshape(panel_rows, B).astype(jnp.float32) + additions).astype(
        jnp.bfloat16
    )
    full_tile = lax.all_gather(diag_tile, ("row", "col"), axis=0, tiled=True)
    pivot_block = full_tile[pivot_order]
    inverse = approximate_inverse(pivot_block)
    panel_full = lax.all_gather(panel_row, "row", axis=3, tiled=True)
    leading = panel_full[:, 0][:, :, pivot_order].astype(jnp.float32) * pattern[
        :, None, None
    ].astype(jnp.float32)
    lead_cols = jnp.transpose(leading, (2, 0, 1)).reshape(B, TC * K)
    images = jnp.dot(inverse, lead_cols, precision=highest_precision).astype(jnp.bfloat16)
    column_factors = panel_full[:, 1]
    spread = jnp.dot(
        corrected,
        lax.all_gather(images, "col", axis=1, tiled=True),
        preferred_element_type=jnp.float32,
    ).astype(jnp.bfloat16)
    spread = spread.reshape(TR, row_block, n_coldev, TC * K)
    landed = lax.all_to_all(spread, "col", split_axis=2, concat_axis=1, tiled=True)
    products = landed.reshape(TR, B, TC, K)
    rank_mask = jnp.arange(K, dtype=jnp.int32)[None, None, :] < tile_ranks[:, :, None]
    left_factors = jnp.where(
        rank_mask[..., None], trail_factors[:, :, 0], jnp.zeros((), jnp.bfloat16)
    )
    right_factors = trail_factors[:, :, 1]

    def tile_row(operands):
        left_row, right_row, product_row = operands
        lowrank = jnp.einsum(
            "jkb,jkc->jbc", left_row, right_row, preferred_element_type=jnp.float32
        )
        change = jnp.einsum(
            "bjk,jkc->jbc", product_row, column_factors, preferred_element_type=jnp.float32
        )
        return (lowrank - change).astype(jnp.bfloat16)

    return lax.map(tile_row, (left_factors, right_factors, products))


def solution(mesh):
    placed = (
        P(("row", "col"), None),
        P(),
        P("row", "col", None),
        P("col", None, None, "row"),
        P("row", "col", None, None, None),
        P("row", "col"),
        P("col"),
        P(("row", "col"), None),
        P(("row", "col"), None),
        P(("row", "col")),
        P(("row", "col")),
    )
    return jax.shard_map(
        per_device,
        mesh=mesh,
        in_specs=placed,
        out_specs=P("row", "col", None, None),
        check_vma=False,
    )
```

profile of v0, /device:TPU:0, one launch (start us, length us, event | category | flops | bytes accessed | tf_op | source)
XLA Modules:
  0.0 239.9 jit_solution(7742414481218553313)
XLA Ops:
  6.5 0.7 all-gather.6.cloned.1.call-update
  7.3 0.0 all-gather.4.cloned.1.call-start
  7.3 1.0 copy.60
  8.3 0.7 compare_select_fusion
  9.0 15.1 %all_gather.10 = bf16[4,2,64,512]{2,0,3,1:T(4,128)(2,1)S(1)} all-gather(bf16[4,2,64,64]{2,0,3,1:T(4,128)(2,1)S(1)} %copy.60), channel_id=1, replica_groups=mesh['row'=8,'col'=16] {'row'}, dimensions={3}, use_global_device_ids=true | all-gather | bytes 589824 | tf_op jit(solution)/shard_map/all_gather | solution.py:82
  24.1 0.4 slice_bitcast_fusion.1
  24.5 2.1 gather_fusion.2
  26.6 0.3 copy.61
  26.9 0.1 convert_multiply_fusion
  27.0 49.2 %all-gather.6.cloned.1.call-done = f32[128,4,512]{2,1,0:T(4,128)} async-done(((f32[1,4,512]{2,1,0:T(4,128)}), f32[128,4,512]{2,1,0:T(4,128)}) %all-gather.6.cloned.1.call-update) | async-done | bytes 1048592 | tf_op jit(solution)/shard_map/all_gather | solution.py:79
  76.2 1.6 reshape.104
  77.8 1.6 gather_fusion
  79.4 4.5 %gather_fusion.1 = f32[512]{0:T(512)S(1)} fusion(f32[512,512]{1,0:T(8,128)S(1)} %gather_fusion, s32[512]{0:T(512)S(1)} %bitcast.70), kind=kCustom, calls=%fused_computation.1 | custom fusion | bytes 8192 | tf_op jit(solution)/shard_map/jit(diagonal)/cond/branch_0_fun/gather | solution.py:17
  83.9 1.8 fusion.11
  85.8 1.8 fusion.13
  87.7 1.8 fusion.44
  89.5 1.9 convolution_subtract_fusion
  91.4 1.7 convolution_convert_fusion.2
  93.8 0.2 convert_reduce_fusion
  94.0 0.3 convolution_convert_fusion.3
  94.4 0.2 reshape.71
  94.6 0.7 copy.57
  95.3 6.3 %all-to-all-start = ((bf16[128,4,2]{1,2,0:T(2,128)(2,1)}), bf16[128,4,2]{1,2,0:T(2,128)(2,1)S(1)}, u32[]{:S(2)}, u32[]{:S(2)}) async-start(bf16[128,4,2]{1,2,0:T(2,128)(2,1)} %copy.57), calls=%async_computation | async-start | bytes 131072 | tf_op jit(solution)/shard_map/all_to_all | solution.py:66
  101.6 0.3 convolution_convert_fusion.1
  101.9 0.9 reshape.72
  102.9 8.1 %all-to-all-done = bf16[128,4,2]{1,2,0:T(2,128)(2,1)S(1)} async-done(((bf16[128,4,2]{1,2,0:T(2,128)(2,1)}), bf16[128,4,2]{1,2,0:T(2,128)(2,1)S(1)}, u32[]{:S(2)}, u32[]{:S(2)}) %all-to-all-start) | async-done | bytes 2080 | tf_op jit(solution)/shard_map/all_to_all | solution.py:66
  110.9 4.7 %all-to-all-start.1 = ((bf16[128,4,512]{2,1,0:T(4,128)(2,1)}), bf16[128,4,512]{2,1,0:T(4,128)(2,1)S(1)}, u32[]{:S(2)}, u32[]{:S(2)}) async-start(bf16[128,4,512]{2,1,0:T(4,128)(2,1)} %reshape.72), calls=%async_computation.1 | async-start | bytes 1048576 | tf_op jit(solution)/shard_map/all_to_all | solution.py:65
  115.6 0.1 copy.58
  115.7 0.1 copy.59
  115.9 0.1 reshape.78
  116.0 13.2 %all-to-all-done.1 = bf16[128,4,512]{2,1,0:T(4,128)(2,1)S(1)} async-done(((bf16[128,4,512]{2,1,0:T(4,128)(2,1)}), bf16[128,4,512]{2,1,0:T(4,128)(2,1)S(1)}, u32[]{:S(2)}, u32[]{:S(2)}) %all-to-all-start.1) | async-done | bytes 524320 | tf_op jit(solution)/shard_map/all_to_all | solution.py:65
  129.2 0.1 reshape.73
  129.3 19.5 %all-gather.4.cloned.1.call-done = bf16[512,4096]{1,0:T(8,128)(2,1)} async-done(((bf16[512,256]{1,0:T(8,128)(2,1)}), bf16[512,4096]{1,0:T(8,128)(2,1)}) %all-gather.4.cloned.1.call-update) | async-done | bytes 4194320 | tf_op jit(solution)/shard_map/all_gather | solution.py:91
  148.9 3.8 %convolution_convert_fusion = bf16[256,4096]{1,0:T(8,128)(2,1)S(1)} fusion(bf16[512,4096]{1,0:T(8,128)(2,1)} %all-gather.4.cloned.1.call-done, bf16[512,512]{1,0:T(8,128)(2,1)S(1)} %reshape.73, bf16[256,512]{1,0:T(8,128)(2,1)} %bitcast.75, s32[512]{0:T(512)S(1)} %bitcast.79, pred[512]{0:T(512)(128)(4,1)S(1)} %compare_reduce_fusion), kind=kOutput, calls=%fused_computation.14 | convolution fusion | flops 1209663488 | bytes 7080448 | tf_op jit(solution)/shard_map/dot_general | solution.py:89
  152.7 0.6 copy.68
  153.3 2.0 copy.62
  155.4 5.0 %all-to-all-start.2 = ((bf16[8,32,16,256]{3,1,0,2:T(8,128)(2,1)}), bf16[8,32,16,256]{3,1,0,2:T(8,128)(2,1)S(1)}, u32[]{:S(2)}, u32[]{:S(2)}) async-start(bf16[8,32,16,256]{3,1,0,2:T(8,128)(2,1)} %copy.62), calls=%async_computation.2 | async-start | bytes 4194304 | tf_op jit(solution)/shard_map/all_to_all | solution.py:95
  160.3 0.3 copy.65
  160.7 0.1 copy.54
  160.7 0.1 iota_compare_fusion.6
  160.8 3.3 %slice_bitcast_fusion = bf16[8,4,64,512]{3,2,1,0:T(8,128)(2,1)} fusion(bf16[8,4,2,64,512]{4,3,2,1,0:T(8,128)(2,1)} %param.17), kind=kLoop, calls=%fused_computation.16 | loop fusion | bytes 4194304 | tf_op jit(solution)/shard_map/squeeze | solution.py:101
  164.1 1.6 bitcast_select_fusion
  165.7 24.4 %all-to-all-done.2 = bf16[8,32,16,256]{3,1,0,2:T(8,128)(2,1)S(1)} async-done(((bf16[8,32,16,256]{3,1,0,2:T(8,128)(2,1)}), bf16[8,32,16,256]{3,1,0,2:T(8,128)(2,1)S(1)}, u32[]{:S(2)}, u32[]{:S(2)}) %all-to-all-start.2) | async-done | bytes 2097184 | tf_op jit(solution)/shard_map/all_to_all | solution.py:95
  190.2 1.3 copy-done.1
  191.5 1.8 copy.63
  193.3 3.2 %reshape.76 = bf16[8,512,4,64]{3,2,1,0:T(4,128)(2,1)} reshape(bf16[8,16,32,1,256]{4,2,1,0,3:T(8,128)(2,1)S(1)} %copy.63) | data formatting | bytes 4194304 | tf_op jit(solution)/shard_map/reshape | solution.py:96
  196.6 5.6 %copy.64 = bf16[8,512,4,64]{1,3,2,0:T(8,128)(2,1)S(1)} copy(bf16[8,512,4,64]{3,2,1,0:T(4,128)(2,1)} %reshape.76) | data formatting | bytes 4194304 | tf_op jit(solution)/shard_map/while | solution.py:113
  202.2 31.0 %while.10 = (s32[]{:T(128)}, bf16[8,4,512,512]{3,2,1,0:T(8,128)(2,1)}, bf16[8,4,64,512]{3,2,1,0:T(8,128)(2,1)}, bf16[8,4,64,512]{3,2,1,0:T(8,128)(2,1)}, bf16[8,...) while((s32[]{:T(128)}, bf16[8,4,512,512]{3,2,1,0:T(8,128)(2,1)}, ...), condition=%wide.region_2.3_spmd, body=%wide.region_1.2_spmd.sunk | while | flops 270532608 | bytes 11536461 | solution.py:113
  202.2 1.8 fusion.66
  204.0 2.1 bitcast_dynamic-update-slice_fusion.2
  206.0 1.8 fusion.66
  207.8 2.1 bitcast_dynamic-update-slice_fusion.2
  209.9 1.8 fusion.66
  211.7 2.1 bitcast_dynamic-update-slice_fusion.2
  213.8 1.8 fusion.66
  215.6 2.1 bitcast_dynamic-update-slice_fusion.2
  217.6 1.8 fusion.66
  219.4 2.1 bitcast_dynamic-update-slice_fusion.2
  221.5 1.8 fusion.66
  223.3 2.1 bitcast_dynamic-update-slice_fusion.2
  225.4 1.8 fusion.66
  227.2 2.1 bitcast_dynamic-update-slice_fusion.2
  229.2 1.8 fusion.66
  231.0 2.1 bitcast_dynamic-update-slice_fusion.2
  (25 shorter events, 0.1 us)
Async XLA Ops:
  6.5 95.1 %copy-start = (bf16[256,512]{1,0:T(8,128)(2,1)S(1)}, bf16[256,512]{1,0:T(8,128)(2,1)}, u32[]{:S(2)}) copy-start(bf16[256,512]{1,0:T(8,128)(2,1)} %param.20) | copy-start | bytes 786436
  6.5 20.3 %copy-start.6 = (s32[4]{0:T(128)S(1)}, s32[4]{0:T(128)}, u32[]{:S(2)}) copy-start(s32[4]{0:T(128)} %param.19) | copy-start | bytes 52
  6.5 69.6 %all-gather.6.cloned.1.call-start = ((), (), s32[]{:S(2)}) async-start(), calls=%async_computation.4 | async-start | bytes 1056768 | tf_op jit(solution)/shard_map/all_gather | solution.py:79
  7.3 141.6 %all-gather.4.cloned.1.call-start = ((), (), s32[]{:S(2)}) async-start(), calls=%async_computation.3 | async-start | bytes 4456448 | tf_op jit(solution)/shard_map/all_gather | solution.py:91
  87.7 6.1 %copy-start.3 = (s32[256,1]{0,1:T(1,128)S(1)}, s32[256,1]{0,1:T(1,128)}, u32[]{:S(2)}) copy-start(s32[256,1]{0,1:T(1,128)} %param.21) | copy-start | bytes 3076
  87.7 6.3 %copy-start.5 = (s32[256]{0:T(256)S(1)}, s32[256]{0:T(256)}, u32[]{:S(2)}) copy-start(s32[256]{0:T(256)} %param.22) | copy-start | bytes 3076
  95.3 15.7 %all-to-all-start = ((bf16[128,4,2]{1,2,0:T(2,128)(2,1)}), bf16[128,4,2]{1,2,0:T(2,128)(2,1)S(1)}, u32[]{:S(2)}, u32[]{:S(2)}) async-start(bf16[128,4,2]{1,2,0:T(2,128)(2,1)} %copy.57), calls=%async_computation | async-start | bytes 131072 | tf_op jit(solution)/shard_map/all_to_all | solution.py:66
  110.9 18.3 %all-to-all-start.1 = ((bf16[128,4,512]{2,1,0:T(4,128)(2,1)}), bf16[128,4,512]{2,1,0:T(4,128)(2,1)S(1)}, u32[]{:S(2)}, u32[]{:S(2)}) async-start(bf16[128,4,512]{2,1,0:T(4,128)(2,1)} %reshape.72), calls=%async_computation.1 | async-start | bytes 1048576 | tf_op jit(solution)/shard_map/all_to_all | solution.py:65
  153.3 7.3 %copy-start.4 = (s32[8,4]{0,1:T(4,128)S(1)}, s32[8,4]{0,1:T(4,128)}, u32[]{:S(2)}) copy-start(s32[8,4]{0,1:T(4,128)} %param.18) | copy-start | bytes 388
  155.4 34.8 %all-to-all-start.2 = ((bf16[8,32,16,256]{3,1,0,2:T(8,128)(2,1)}), bf16[8,32,16,256]{3,1,0,2:T(8,128)(2,1)S(1)}, u32[]{:S(2)}, u32[]{:S(2)}) async-start(bf16[8,32,16,256]{3,1,0,2:T(8,128)(2,1)} %copy.62), calls=%async_computation.2 | async-start | bytes 4194304 | tf_op jit(solution)/shard_map/all_to_all | solution.py:95
  160.7 3.4 %copy-start.2 = (bf16[8,4,2,64,512]{4,3,2,1,0:T(8,128)(2,1)S(1)}, bf16[8,4,2,64,512]{4,3,2,1,0:T(8,128)(2,1)}, u32[]{:S(2)}) copy-start(bf16[8,4,2,64,512]{4,3,2,1,0:T(8,128)(2,1)} %param.17) | copy-start | bytes 12582916
  190.2 1.3 copy-start.1
Sparse Core Ops, SparseCore 0:
  10.1 65.9 all-gather.5
  93.3 55.5 all-gather.3
where the time goes:
time: 241 us; the launch traced here: 240 us
  waiting for transfers between devices  115 us (48%)
  matrix products  44.4 us (18%)
  local copies, waits for them, and re-layouts  32.2 us (13%)
  starting transfers between devices  16 us (7%)
  blocking collectives  15.1 us (6%)
  between operations  14.3 us (6%)
  other arithmetic  2.71 us (1%)
    all_gather x1, waiting for transfers between devices, per_device(): full_tile = lax.all_gather(diag_tile, ('row', 'col'), axis=0, tiled=True)  49.2 us
    all_to_all x1, waiting for transfers between devices, per_device(): lax.all_to_all(spread, 'col', split_axis=2, concat_axis=1, tiled=True)  24.4 us
    all_gather x1, waiting for transfers between devices, per_device(): lax.all_gather(images, 'col', axis=1, tiled=True)  19.5 us
    dot_general x8, matrix products, tile_row(): jnp.einsum('bjk,jkc->jbc', product_row, column_factors, preferred_element...  16.7 us
    all_gather x1, blocking collectives, per_device(): panel_full = lax.all_gather(panel_row, 'row', axis=3, tiled=True)  15.1 us
    dot_general x8, matrix products, tile_row(): jnp.einsum('jkb,jkc->jbc', left_row, right_row, preferred_element_type=jn...  14.2 us
    all_to_all x1, waiting for transfers between devices, per_device(): lax.all_to_all(flat_vals, ('row', 'col'), split_axis=0, concat_axis=0, ti...  13.2 us
    all_to_all x1, waiting for transfers between devices, per_device(): lax.all_to_all(flat_index, ('row', 'col'), split_axis=0, concat_axis=0, t...  8.05 us
  transfers between devices with their start and end apart: 5, of which 5 were waited for; matrix products, arithmetic and copies ran while one was open for 5% of the time, Pallas kernels for 0%

commit v1 on v0

v1 whole, which is shorter than its diff:
```python
import jax
import jax.numpy as jnp
from jax import lax
from jax.experimental import pallas as pl
from jax.experimental.pallas import tpu as pltpu
from jax.sharding import PartitionSpec as P

B = 512
K = 64
TR = 8
TC = 4
NEAR = 256
CAP = 4
RB = 32
N_ROW = 8
N_COL = 16
N_DEV = 128
MESH = pl.DeviceIdType.MESH
F32 = jnp.float32
BF16 = jnp.bfloat16
NN = (((1,), (0,)), ((), ()))
NT = (((1,), (1,)), ((), ()))
TN = (((0,), (0,)), ((), ()))


def dot(a, b, dims):
    return lax.dot_general(a, b, dims, preferred_element_type=F32)


def iota(shape, dim):
    return lax.broadcasted_iota(jnp.int32, shape, dim)


def split(a):
    high = a.astype(BF16)
    return high, (a - high.astype(F32)).astype(BF16)


def halves_dot(a, b_high, b_low, dims):
    a_high, a_low = split(a)
    return dot(a_high, b_high, dims) + (dot(a_high, b_low, dims) + dot(a_low, b_high, dims))


def exchange_kernel(
    near_vals,
    near_dest,
    near_row,
    near_count,
    panel_col,
    diag_tile,
    pivot_order,
    panel_row,
    pattern,
    products,
    neg_v,
    near_out,
    near_in,
    meta_own,
    meta_row,
    meta_all,
    diag_x,
    diag_all,
    panel_all,
    grid,
    one_send,
    one_recv,
    ring_send,
    ring_recv,
):
    row = lax.axis_index("row")
    col = lax.axis_index("col")
    y, x = col // 4, lax.rem(col, 4)
    z, core = row // 2, lax.rem(row, 2)
    me = row * N_COL + col
    me_in = col * N_ROW + row

    def up(v):
        return lax.rem(v + 1, 4)

    def down(v):
        return lax.rem(v + 3, 4)

    barrier = pltpu.get_barrier_semaphore()

    def greet(step, carry):
        other = lax.rem(me + step, N_DEV)
        pl.semaphore_signal(
            barrier, inc=1, device_id=(other // N_COL, lax.rem(other, N_COL)), device_id_type=MESH
        )
        return carry

    lax.fori_loop(1, N_DEV, greet, 0)

    def copy(src, dst, sems, device):
        return pltpu.make_async_remote_copy(
            src_ref=src,
            dst_ref=dst,
            send_sem=sems[0],
            recv_sem=sems[1],
            device_id=device,
            device_id_type=MESH,
        )

    dest_col = near_dest[...]
    eye = iota((NEAR, NEAR), 0) == iota((NEAR, NEAR), 1)
    dest_lane = jnp.sum(jnp.where(eye, dest_col, 0), axis=0, keepdims=True)
    row_col = jnp.sum(jnp.where(eye, near_row[...], 0), axis=1, keepdims=True)
    earlier = (dest_col == dest_lane) & (iota((NEAR, NEAR), 1) < iota((NEAR, NEAR), 0))
    position = jnp.sum(jnp.where(earlier, 1, 0), axis=1, keepdims=True)
    live = iota((NEAR, 1), 0) < near_count[0]
    slot = jnp.where(live, dest_col * CAP + position, -1)
    placing = slot == iota((NEAR, N_DEV * CAP), 1)
    table = jnp.sum(jnp.where(placing, (row_col + 1).astype(F32), 0.0), axis=0, keepdims=True)
    placed = dot(jnp.where(placing, 1.0, 0.0).astype(BF16), near_vals[...], TN)
    low = iota((64, 8, 128), 1) < 4
    pieces = [placed[:, 128 * b : 128 * b + 128].reshape(64, 8, 128) for b in range(4)]
    turned = [pltpu.roll(p, 4, 1) for p in pieces]
    even = jnp.concatenate(
        [jnp.where(low, pieces[0], turned[1]), jnp.where(low, pieces[2], turned[3])], axis=1
    )
    odd = jnp.concatenate(
        [jnp.where(low, turned[0], pieces[1]), jnp.where(low, turned[2], pieces[3])], axis=1
    )
    both = jnp.concatenate([even[:, None], odd[:, None]], axis=1)
    near_out[...] = both.reshape(N_DEV, 16, 128).astype(BF16)

    meta = jnp.zeros((32, 128), F32)
    for m in range(4):
        meta = meta + jnp.where(
            iota((32, 128), 0) == 4 * row + m, table[:, 128 * m : 128 * m + 128], 0.0
        )
    meta_own[...] = meta.astype(BF16)

    own_rows = diag_tile[...]
    diag_x[x] = jnp.where(
        iota((16, B), 0) // 4 == x, jnp.concatenate([own_rows] * 4, axis=0), 0.0
    )
    panel_all[z, core] = panel_row[...]

    pl.semaphore_wait(barrier, N_DEV - 1)

    ones = iter(range(64))

    def sems():
        k = next(ones)
        return one_send.at[k], one_recv.at[k]

    def finish(copies):
        for c in copies:
            c.wait_recv()

    started = []

    def begin(copies):
        for c in copies:
            c.start()
        started.extend(copies)

    meta_row_copies = []
    for k in range(1, N_ROW):
        meta_row_copies.append(
            copy(meta_own, meta_row.at[k], sems(), (lax.rem(row + k, N_ROW), col))
        )
    begin(meta_row_copies)
    diag_x_copies = [
        copy(diag_x.at[x], diag_x.at[x], sems(), (row, 4 * y + lax.rem(x + k, 4))) for k in (1, 3, 2)
    ]
    begin(diag_x_copies)

    near_sems = sems()

    def send_near(step, carry):
        other = lax.rem(me + step, N_DEV)
        copy(
            near_out.at[other],
            near_in.at[me_in],
            near_sems,
            (other // N_COL, lax.rem(other, N_COL)),
        ).start()
        return carry

    lax.fori_loop(1, N_DEV, send_near, 0)
    near_in[me_in] = near_out[me]

    finish(meta_row_copies)
    total = meta_own[...].astype(F32)
    for k in range(1, N_ROW):
        total = total + meta_row[k].astype(F32)
    meta_all[col] = total.astype(BF16)
    meta_copies = [
        copy(meta_all.at[col], meta_all.at[col], sems(), (row, lax.rem(col + k, N_COL)))
        for k in range(1, N_COL)
    ]
    begin(meta_copies)

    finish(diag_x_copies)
    mine = diag_all.at[z, core, pl.ds(pl.multiple_of(16 * y, 16), 16)]
    mine[...] = (diag_x[0] + diag_x[1]) + (diag_x[2] + diag_x[3])
    diag_y_copies = [copy(mine, mine, sems(), (row, 4 * lax.rem(y + k, 4) + x)) for k in (1, 3, 2)]
    begin(diag_y_copies)

    panel_z_copies = [
        copy(
            panel_all.at[z, core],
            panel_all.at[z, core],
            sems(),
            (2 * lax.rem(z + k, 4) + core, col),
        )
        for k in (1, 3, 2)
    ]
    begin(panel_z_copies)

    wide_eye = iota((B, B), 0) == iota((B, B), 1)
    pivot_col = jnp.sum(jnp.where(wide_eye, pivot_order[...], 0), axis=1, keepdims=True)
    pivoting = jnp.where(pivot_col == iota((B, B), 1), 1.0, 0.0).astype(BF16)

    finish(meta_copies)
    slots = N_DEV * CAP
    ids = iota((slots, 1), 0)
    wanted = (ids // CAP) * CAP + me // 32
    choose = jnp.where(iota((slots, slots), 1) == wanted, 1.0, 0.0).astype(BF16)
    named = dot(choose, meta_all[...].reshape(slots, 128), NN)
    lane = lax.rem(me, 32) * CAP + lax.rem(ids, CAP)
    target = jnp.sum(jnp.where(iota((slots, 128), 1) == lane, named, 0.0), axis=1, keepdims=True)
    landing = jnp.where(target.astype(jnp.int32) - 1 == iota((slots, 256), 1), 1.0, 0.0).astype(BF16)

    finish(diag_y_copies)
    diag_z_copies = [
        copy(
            diag_all.at[z, core],
            diag_all.at[z, core],
            sems(),
            (2 * lax.rem(z + k, 4) + core, col),
        )
        for k in (1, 3, 2)
    ]
    begin(diag_z_copies)

    near_all = near_in.at[pl.ds(0, N_DEV - 1)]
    pltpu.make_async_copy(near_all, near_all, near_sems[1]).wait()
    both = near_in[...].astype(F32).reshape(64, 2, 16, 128)
    even, odd = both[:, 0], both[:, 1]
    columns = []
    for b in range(0, 4, 2):
        first, second = even[:, 4 * b : 4 * b + 8], odd[:, 4 * b : 4 * b + 8]
        columns.append(jnp.where(low, first, pltpu.roll(second, 4, 1)).reshape(slots, 128))
        columns.append(jnp.where(low, pltpu.roll(first, 4, 1), second).reshape(slots, 128))
    arrived = jnp.concatenate(columns, axis=1).astype(BF16)
    additions = dot(landing, arrived, TN)
    corrected = (panel_col[...].astype(F32) + additions.reshape(TR, RB, B)).astype(BF16)
    for i in range(TR):
        grid[i, y, x] = corrected[i]

    def ring_copy(i, phase, k, part, device):
        return copy(part, part, (ring_send.at[i, phase, k], ring_recv.at[i, phase, k]), device)

    def first_phase(i):
        if i % 2 == 0:
            plus, minus = (row, 4 * y + up(x)), (row, 4 * y + down(x))
            before, after = grid.at[i, y, down(x)], grid.at[i, y, up(x)]
        else:
            plus, minus = (row, 4 * up(y) + x), (row, 4 * down(y) + x)
            before, after = grid.at[i, down(y), x], grid.at[i, up(y), x]
        own = grid.at[i, y, x]
        return (
            ring_copy(i, 0, 0, own, plus),
            ring_copy(i, 0, 1, own, minus),
            ring_copy(i, 0, 2, before.at[pl.ds(0, 16)], plus),
            ring_copy(i, 0, 3, after.at[pl.ds(16, 16)], minus),
        )

    def second_phase(i):
        if i % 2 == 0:
            plus, minus = (row, 4 * up(y) + x), (row, 4 * down(y) + x)
            own = grid.at[i, y]
            before, after = grid.at[i, down(y), pl.ds(0, 2)], grid.at[i, up(y), pl.ds(2, 2)]
        else:
            plus, minus = (row, 4 * y + up(x)), (row, 4 * y + down(x))
            own = grid.at[i, :, x]
            before, after = grid.at[i, pl.ds(0, 2), down(x)], grid.at[i, pl.ds(2, 2), up(x)]
        return (
            ring_copy(i, 1, 0, own, plus),
            ring_copy(i, 1, 1, own, minus),
            ring_copy(i, 1, 2, before, plus),
            ring_copy(i, 1, 3, after, minus),
        )

    one = [first_phase(i) for i in range(TR)]
    two = [second_phase(i) for i in range(TR)]
    for i in range(TR):
        begin(one[i][:2])

    finish(panel_z_copies + diag_z_copies)
    partner = (2 * z + 1 - core, col)
    core_copies = [
        copy(diag_all.at[:, core], diag_all.at[:, core], sems(), partner),
        copy(panel_all.at[:, core], panel_all.at[:, core], sems(), partner),
    ]
    begin(core_copies)

    for i in range(TR):
        one[i][0].wait_recv()
        begin([one[i][2]])
        one[i][1].wait_recv()
        begin([one[i][3]])
    for i in range(TR):
        finish(one[i][2:])
        begin(two[i][:2])

    finish(core_copies)
    tile = diag_all[...].reshape(B, B)
    high, low_part = split(tile)
    pivot_high = dot(pivoting, high, NN)
    pivot_low = dot(pivoting, low_part, NN)
    scale = 1.0 / jnp.sum(jnp.where(wide_eye, pivot_high + pivot_low, 0.0), axis=0, keepdims=True)
    pivot_high, pivot_low = pivot_high.astype(BF16), pivot_low.astype(BF16)
    left = jnp.concatenate(
        [panel_all[a, b, :, 0].reshape(TC * K, 64) for a in range(4) for b in range(2)], axis=1
    )
    neg_v[...] = -jnp.concatenate(
        [panel_all[a, b, :, 1].reshape(TC * K, 64) for a in range(4) for b in range(2)], axis=1
    )
    lead = dot(left, pivoting, NT)
    kept = jnp.concatenate(
        [jnp.full((K, 1), pattern[j].astype(F32), F32) for j in range(TC)], axis=0
    )
    lead = lead * kept

    def through_pivot(a):
        return halves_dot(a, pivot_high, pivot_low, NT)

    def once(a):
        scaled = a * scale
        return 2.0 * scaled - through_pivot(scaled) * scale

    inner = once(lead)
    images = (2.0 * inner - once(through_pivot(inner))).astype(BF16)

    for i in range(TR):
        two[i][0].wait_recv()
        begin([two[i][2]])
        two[i][1].wait_recv()
        begin([two[i][3]])
    for i in range(TR):
        finish(two[i][2:])
        products[i] = dot(images, grid[i].reshape(B, B), NT).astype(BF16)

    for c in started:
        c.wait_send()
    pltpu.make_async_copy(near_all, near_all, near_sems[0]).wait()


def exchange(*operands):
    vmem = pl.BlockSpec(memory_space=pltpu.VMEM)
    smem = pl.BlockSpec(memory_space=pltpu.SMEM)
    dma = pltpu.SemaphoreType.DMA
    return pl.pallas_call(
        exchange_kernel,
        out_shape=(
            jax.ShapeDtypeStruct((TR, TC * K, B), BF16),
            jax.ShapeDtypeStruct((TC * K, B), BF16),
        ),
        in_specs=[vmem, vmem, vmem, smem, vmem, vmem, vmem, vmem, smem],
        out_specs=(vmem, vmem),
        scratch_shapes=[
            pltpu.VMEM((N_DEV, 16, 128), BF16),
            pltpu.VMEM((N_DEV, 16, 128), BF16),
            pltpu.VMEM((32, 128), BF16),
            pltpu.VMEM((8, 32, 128), BF16),
            pltpu.VMEM((16, 32, 128), BF16),
            pltpu.VMEM((4, 16, B), F32),
            pltpu.VMEM((4, 2, 64, B), F32),
            pltpu.VMEM((4, 2, TC, 2, K, 64), BF16),
            pltpu.VMEM((TR, 4, 4, RB, B), BF16),
            dma((48,)),
            dma((48,)),
            dma((TR, 2, 4)),
            dma((TR, 2, 4)),
        ],
        compiler_params=pltpu.CompilerParams(
            collective_id=0, has_side_effects=True, vmem_limit_bytes=56 << 20
        ),
    )(*operands)


def update_kernel(ranks, trail, products, neg_v, out):
    i = pl.program_id(0)
    half = pl.program_id(1)
    for j in range(2):
        rank = ranks[i, half * 2 + j]
        left = jnp.where(iota((K, B), 0) < rank, trail[0, j, 0], jnp.zeros((), BF16))
        rows = pl.ds(K * j, K)
        lhs = jnp.concatenate([left, products[0, rows]], axis=0)
        rhs = jnp.concatenate([trail[0, j, 1], neg_v[rows]], axis=0)
        out[0, j] = dot(lhs, rhs, TN).astype(BF16)


def update(ranks, trail, products, neg_v):
    return pl.pallas_call(
        update_kernel,
        grid=(TR, 2),
        out_shape=jax.ShapeDtypeStruct((TR, TC, B, B), BF16),
        in_specs=[
            pl.BlockSpec(memory_space=pltpu.SMEM),
            pl.BlockSpec((1, 2, 2, K, B), lambda i, h: (i, h, 0, 0, 0)),
            pl.BlockSpec((1, 2 * K, B), lambda i, h: (i, h, 0)),
            pl.BlockSpec((2 * K, B), lambda i, h: (h, 0)),
        ],
        out_specs=pl.BlockSpec((1, 2, B, B), lambda i, h: (i, h, 0, 0)),
        compiler_params=pltpu.CompilerParams(vmem_limit_bytes=32 << 20),
    )(ranks, trail, products, neg_v)


def per_device(
    diag_tile,
    pivot_order,
    panel_col,
    panel_row,
    trail_factors,
    tile_ranks,
    pattern,
    near_vals,
    near_dest,
    near_row,
    near_count,
):
    products, neg_v = exchange(
        near_vals,
        near_dest,
        near_row.reshape(1, NEAR),
        near_count,
        panel_col,
        diag_tile,
        pivot_order.reshape(1, B),
        panel_row,
        pattern,
    )
    return update(tile_ranks, trail_factors, products, neg_v)


def solution(mesh):
    placed = (
        P(("row", "col"), None),
        P(),
        P("row", "col", None),
        P("col", None, None, "row"),
        P("row", "col", None, None, None),
        P("row", "col"),
        P("col"),
        P(("row", "col"), None),
        P(("row", "col"), None),
        P(("row", "col")),
        P(("row", "col")),
    )
    return jax.shard_map(
        per_device,
        mesh=mesh,
        in_specs=placed,
        out_specs=P("row", "col", None, None),
        check_vma=False,
    )
```

time: 241 us -> 79.3 us (0.33)
  waiting for transfers between devices: 115 us -> 0 us
  Pallas kernels: 0 us -> 71.4 us
  matrix products: 44.4 us -> 0 us
  local copies, waits for them, and re-layouts: 32.2 us -> 6.95 us
  starting transfers between devices: 16 us -> 0 us
  blocking collectives: 15.1 us -> 0 us
  between operations: 14.3 us -> 0.67 us
  other arithmetic: 2.71 us -> 0 us
    pallas_call x0 -> x2, Pallas kernels: none -> 71.4 us  [the longest x1 58.7 us: exchange(): pl.pallas_call(exchange_kernel, out_shape=(jax.ShapeDtypeStruct((TR, TC *...]
    all_gather x2 -> x0, waiting for transfers between devices: 68.7 us -> none  [the longest x1 49.2 us: per_device(): full_tile = lax.all_gather(diag_tile, ('row', 'col'), axis=0, tiled=True)]
    all_to_all x3 -> x0, waiting for transfers between devices: 45.7 us -> none  [the longest x1 24.4 us: per_device(): lax.all_to_all(spread, 'col', split_axis=2, concat_axis=1, tiled=True)]
    dot_general x24 -> x0, matrix products: 44.4 us -> none  [the longest x8 16.7 us: tile_row(): jnp.einsum('bjk,jkc->jbc', product_row, column_factors, preferred_element...]
    all_to_all x3 -> x0, starting transfers between devices: 16 us -> none  [the longest x1 6.35 us: per_device(): lax.all_to_all(flat_index, ('row', 'col'), split_axis=0, concat_axis=0, t...]
    all_gather x1 -> x0, blocking collectives: 15.1 us -> none  [per_device(): panel_full = lax.all_gather(panel_row, 'row', axis=3, tiled=True)]
    gather x4 -> x0, local copies, waits for them, and re-layouts: 8.53 us -> none  [the longest x1 4.52 us: approximate_inverse(): inverse = jnp.diag(1.0 / jnp.diagonal(pivot_block))]
    reshape x6 -> x0, local copies, waits for them, and re-layouts: 7.23 us -> none  [the longest x1 3.25 us: per_device(): products = landed.reshape(TR, B, TC, K)]
  transfers between devices with their start and end apart: 5 -> 0, of which waited for: 5 -> 0; matrix products, arithmetic and copies ran while one was open for 5% -> 0% of each run, Pallas kernels for 0% -> 0%
where the time goes in v1:
time: 79.3 us; the launch traced here: 79 us
  Pallas kernels  71.4 us (90%)
  local copies, waits for them, and re-layouts  6.95 us (9%)
    pallas_call x1, Pallas kernels, exchange(): pl.pallas_call(exchange_kernel, out_shape=(jax.ShapeDtypeStruct((TR, TC *...  58.7 us
    pallas_call x1, Pallas kernels, update(): pl.pallas_call(update_kernel, grid=(TR, 2), out_shape=jax.ShapeDtypeStruc...  12.7 us
    unnamed x8, local copies, waits for them, and re-layouts  6.95 us

profile of v1, /device:TPU:0, one launch (start us, length us, event | category | flops | bytes accessed | tf_op | source)
XLA Modules:
  0.0 79.0 jit_solution(15533030378710535466)
XLA Ops:
  0.7 0.8 copy.13.ranks
  1.4 1.5 %copy.12.near_dest = s32[256,1]{1,0:T(8,128)} copy(s32[256,1]{0,1:T(1,128)} %param.19) | data formatting | bytes 2048 | tf_op args[8]
  2.9 58.7 %shard_map.109 = (bf16[8,256,512]{2,1,0:T(8,128)(2,1)}, bf16[256,512]{1,0:T(8,128)(2,1)}) custom-call(bf16[256,512]{1,0:T(8,128)(2,1)} %near_vals.1, s32[256,1]{1,0:T(8,128)} %copy.12.near_dest, s32[1,256]{1,0:T(1,128)} %bitcast.3, s32[1]{0:T(128)S(6)} %copy.14.near_count, bf16[8,32,512]{2,1,0:T(8,128)(2,1)} %panel_col.1, f32[4,512]{1,0:T(4,128)} %diag_tile.1, ...), custom_call_target="tpu_custom_call" | custom-call | tf_op jit(solution)/shard_map/pallas_call | solution.py:357
  61.6 0.0 copy-start
  61.6 2.2 %copy-done = bf16[8,4,2,64,512]{4,3,2,1,0:T(8,128)(2,1)S(1)} copy-done((bf16[8,4,2,64,512]{4,3,2,1,0:T(8,128)(2,1)S(1)}, bf16[8,4,2,64,512]{4,3,2,1,0:T(8,128)(2,1)}, u32[]{:S(2)}) %copy-start) | copy-done | bytes 4194328
  63.8 0.0 copy-start.1
  63.8 1.6 %copy-done.1 = bf16[8,256,512]{2,1,0:T(8,128)(2,1)S(1)} copy-done((bf16[8,256,512]{2,1,0:T(8,128)(2,1)S(1)}, bf16[8,256,512]{2,1,0:T(8,128)(2,1)}, u32[]{:S(2)}) %copy-start.1) | copy-done | bytes 2097176
  65.4 0.0 copy-start.2
  65.4 0.9 %copy-done.2 = bf16[256,512]{1,0:T(8,128)(2,1)S(1)} copy-done((bf16[256,512]{1,0:T(8,128)(2,1)S(1)}, bf16[256,512]{1,0:T(8,128)(2,1)}, u32[]{:S(2)}) %copy-start.2) | copy-done | bytes 262168
  66.3 12.7 %shard_map.110 = bf16[8,4,512,512]{3,2,1,0:T(8,128)(2,1)} custom-call(s32[8,4]{1,0:T(8,128)S(1)} %copy.13.ranks, bf16[8,4,2,64,512]{4,3,2,1,0:T(8,128)(2,1)S(1)} %copy-done, bf16[8,256,512]{2,1,0:T(8,128)(2,1)S(1)} %copy-done.1, bf16[256,512]{1,0:T(8,128)(2,1)S(1)} %copy-done.2), custom_call_target="tpu_custom_call" | custom-call | tf_op jit(solution)/shard_map/pallas_call | solution.py:399
Async XLA Ops:
  61.6 2.2 %copy-start = (bf16[8,4,2,64,512]{4,3,2,1,0:T(8,128)(2,1)S(1)}, bf16[8,4,2,64,512]{4,3,2,1,0:T(8,128)(2,1)}, u32[]{:S(2)}) copy-start(bf16[8,4,2,64,512]{4,3,2,1,0:T(8,128)(2,1)} %trail.1) | copy-start | bytes 12582916
  63.8 1.6 %copy-start.1 = (bf16[8,256,512]{2,1,0:T(8,128)(2,1)S(1)}, bf16[8,256,512]{2,1,0:T(8,128)(2,1)}, u32[]{:S(2)}) copy-start(bf16[8,256,512]{2,1,0:T(8,128)(2,1)} %get-tuple-element.7.products) | copy-start | bytes 6291460
  65.4 0.9 %copy-start.2 = (bf16[256,512]{1,0:T(8,128)(2,1)S(1)}, bf16[256,512]{1,0:T(8,128)(2,1)}, u32[]{:S(2)}) copy-start(bf16[256,512]{1,0:T(8,128)(2,1)} %get-tuple-element.8.neg_v) | copy-start | bytes 786436

commit v2 on v1

--- a/solution.py
+++ b/solution.py
@@ -15,6 +15,7 @@
 N_ROW = 8
 N_COL = 16
 N_DEV = 128
+N_IN = 10
 MESH = pl.DeviceIdType.MESH
 F32 = jnp.float32
 BF16 = jnp.bfloat16
@@ -41,18 +42,11 @@
     return dot(a_high, b_high, dims) + (dot(a_high, b_low, dims) + dot(a_low, b_high, dims))
 
 
-def exchange_kernel(
-    near_vals,
-    near_dest,
-    near_row,
-    near_count,
-    panel_col,
-    diag_tile,
-    pivot_order,
-    panel_row,
-    pattern,
-    products,
-    neg_v,
+def exchange_kernel(near_count, *refs):
+    sources, (lefts, rights) = refs[:N_IN], refs[N_IN : N_IN + 2]
+    held, local_sems = refs[N_IN + 2 : 2 * N_IN + 1], refs[2 * N_IN + 1]
+    near_dest, near_row, near_vals, diag_tile, panel_row, pivot_order, pattern, panel_col, ranks = held
+    (
     near_out,
     near_in,
     meta_own,
@@ -66,7 +60,17 @@
     one_recv,
     ring_send,
     ring_recv,
-):
+    ) = refs[2 * N_IN + 2 :]
+    loads = [
+        pltpu.make_async_copy(source, place, local_sems.at[k])
+        for k, (source, place) in enumerate(zip(sources, held))
+    ]
+    trail = sources[-1]
+    loads.append(pltpu.make_async_copy(trail.at[:, :, 0], lefts.at[:, :, pl.ds(0, K)], local_sems.at[N_IN]))
+    loads.append(pltpu.make_async_copy(trail.at[:, :, 1], rights.at[:, :, pl.ds(0, K)], local_sems.at[N_IN + 1]))
+    for load in loads:
+        load.start()
+
     row = lax.axis_index("row")
     col = lax.axis_index("col")
     y, x = col // 4, lax.rem(col, 4)
@@ -101,9 +105,12 @@
             device_id_type=MESH,
         )
 
-    dest_col = near_dest[...]
+    for load in loads[:3]:
+        load.wait()
+
+    dest_lane = near_dest[...]
     eye = iota((NEAR, NEAR), 0) == iota((NEAR, NEAR), 1)
-    dest_lane = jnp.sum(jnp.where(eye, dest_col, 0), axis=0, keepdims=True)
+    dest_col = jnp.sum(jnp.where(eye, dest_lane, 0), axis=1, keepdims=True)
     row_col = jnp.sum(jnp.where(eye, near_row[...], 0), axis=1, keepdims=True)
     earlier = (dest_col == dest_lane) & (iota((NEAR, NEAR), 1) < iota((NEAR, NEAR), 0))
     position = jnp.sum(jnp.where(earlier, 1, 0), axis=1, keepdims=True)
@@ -131,6 +138,9 @@
         )
     meta_own[...] = meta.astype(BF16)
 
+    for load in loads[3:9]:
+        load.wait()
+
     own_rows = diag_tile[...]
     diag_x[x] = jnp.where(
         iota((16, B), 0) // 4 == x, jnp.concatenate([own_rows] * 4, axis=0), 0.0
@@ -199,21 +209,6 @@
     diag_y_copies = [copy(mine, mine, sems(), (row, 4 * lax.rem(y + k, 4) + x)) for k in (1, 3, 2)]
     begin(diag_y_copies)
 
-    panel_z_copies = [
-        copy(
-            panel_all.at[z, core],
-            panel_all.at[z, core],
-            sems(),
-            (2 * lax.rem(z + k, 4) + core, col),
-        )
-        for k in (1, 3, 2)
-    ]
-    begin(panel_z_copies)
-
-    wide_eye = iota((B, B), 0) == iota((B, B), 1)
-    pivot_col = jnp.sum(jnp.where(wide_eye, pivot_order[...], 0), axis=1, keepdims=True)
-    pivoting = jnp.where(pivot_col == iota((B, B), 1), 1.0, 0.0).astype(BF16)
-
     finish(meta_copies)
     slots = N_DEV * CAP
     ids = iota((slots, 1), 0)
@@ -225,17 +220,6 @@
     landing = jnp.where(target.astype(jnp.int32) - 1 == iota((slots, 256), 1), 1.0, 0.0).astype(BF16)
 
     finish(diag_y_copies)
-    diag_z_copies = [
-        copy(
-            diag_all.at[z, core],
-            diag_all.at[z, core],
-            sems(),
-            (2 * lax.rem(z + k, 4) + core, col),
-        )
-        for k in (1, 3, 2)
-    ]
-    begin(diag_z_copies)
-
     near_all = near_in.at[pl.ds(0, N_DEV - 1)]
     pltpu.make_async_copy(near_all, near_all, near_sems[1]).wait()
     both = near_in[...].astype(F32).reshape(64, 2, 16, 128)
@@ -289,7 +273,43 @@
     two = [second_phase(i) for i in range(TR)]
     for i in range(TR):
         begin(one[i][:2])
-
+    diag_z_copies = [
+        copy(
+            diag_all.at[z, core],
+            diag_all.at[z, core],
+            sems(),
+            (2 * lax.rem(z + k, 4) + core, col),
+        )
+        for k in (1, 3, 2)
+    ]
+    begin(diag_z_copies)
+
+    panel_z_copies = [
+        copy(
+            panel_all.at[z, core],
+            panel_all.at[z, core],
+            sems(),
+            (2 * lax.rem(z + k, 4) + core, col),
+        )
+        for k in (1, 3, 2)
+    ]
+    begin(panel_z_copies)
+
+
+    for i in range(TR):
+        one[i][0].wait_recv()
+        begin([one[i][2]])
+        one[i][1].wait_recv()
+        begin([one[i][3]])
+    for i in range(TR):
+        finish(one[i][2:])
+        begin(two[i][:2])
+
+    for i in range(0, 4):
+        two[i][0].wait_recv()
+        begin([two[i][2]])
+        two[i][1].wait_recv()
+        begin([two[i][3]])
     finish(panel_z_copies + diag_z_copies)
     partner = (2 * z + 1 - core, col)
     core_copies = [
@@ -298,14 +318,15 @@
     ]
     begin(core_copies)
 
-    for i in range(TR):
-        one[i][0].wait_recv()
-        begin([one[i][2]])
-        one[i][1].wait_recv()
-        begin([one[i][3]])
-    for i in range(TR):
-        finish(one[i][2:])
-        begin(two[i][:2])
+    wide_eye = iota((B, B), 0) == iota((B, B), 1)
+    pivot_col = jnp.sum(jnp.where(wide_eye, pivot_order[...], 0), axis=1, keepdims=True)
+    pivoting = jnp.where(pivot_col == iota((B, B), 1), 1.0, 0.0).astype(BF16)
+
+    for i in range(4, 8):
+        two[i][0].wait_recv()
+        begin([two[i][2]])
+        two[i][1].wait_recv()
+        begin([two[i][3]])
 
     finish(core_copies)
     tile = diag_all[...].reshape(B, B)
@@ -317,14 +338,14 @@
     left = jnp.concatenate(
         [panel_all[a, b, :, 0].reshape(TC * K, 64) for a in range(4) for b in range(2)], axis=1
     )
-    neg_v[...] = -jnp.concatenate(
+    neg_v = -jnp.concatenate(
         [panel_all[a, b, :, 1].reshape(TC * K, 64) for a in range(4) for b in range(2)], axis=1
     )
     lead = dot(left, pivoting, NT)
     kept = jnp.concatenate(
-        [jnp.full((K, 1), pattern[j].astype(F32), F32) for j in range(TC)], axis=0
-    )
-    lead = lead * kept
+        [jnp.broadcast_to(pattern[:, j : j + 1], (K, 1)) for j in range(TC)], axis=0
+    )
+    lead = lead * kept.astype(F32)
 
     def through_pivot(a):
         return halves_dot(a, pivot_high, pivot_low, NT)
@@ -336,33 +357,40 @@
     inner = once(lead)
     images = (2.0 * inner - once(through_pivot(inner))).astype(BF16)
 
-    for i in range(TR):
-        two[i][0].wait_recv()
-        begin([two[i][2]])
-        two[i][1].wait_recv()
-        begin([two[i][3]])
+    for load in loads[9:]:
+        load.wait()
+    for i in range(TR):
+        for j in range(TC):
+            kept = iota((K, B), 0) < ranks[j : j + 1, i : i + 1]
+            lefts[i, j, 0:K] = jnp.where(kept, lefts[i, j, 0:K], jnp.zeros((), BF16))
+            rights[i, j, K : 2 * K] = neg_v[K * j : K * j + K]
+
     for i in range(TR):
         finish(two[i][2:])
-        products[i] = dot(images, grid[i].reshape(B, B), NT).astype(BF16)
+        product = dot(images, grid[i].reshape(B, B), NT).astype(BF16)
+        for j in range(TC):
+            lefts[i, j, K : 2 * K] = product[K * j : K * j + K]
 
     for c in started:
         c.wait_send()
     pltpu.make_async_copy(near_all, near_all, near_sems[0]).wait()
 
 
-def exchange(*operands):
+def exchange(near_count, *operands):
     vmem = pl.BlockSpec(memory_space=pltpu.VMEM)
-    smem = pl.BlockSpec(memory_space=pltpu.SMEM)
+    hbm = pl.BlockSpec(memory_space=pltpu.HBM)
     dma = pltpu.SemaphoreType.DMA
     return pl.pallas_call(
         exchange_kernel,
         out_shape=(
-            jax.ShapeDtypeStruct((TR, TC * K, B), BF16),
-            jax.ShapeDtypeStruct((TC * K, B), BF16),
+            jax.ShapeDtypeStruct((TR, TC, 2 * K, B), BF16),
+            jax.ShapeDtypeStruct((TR, TC, 2 * K, B), BF16),
         ),
-        in_specs=[vmem, vmem, vmem, smem, vmem, vmem, vmem, vmem, smem],
+        in_specs=[pl.BlockSpec(memory_space=pltpu.SMEM)] + [hbm] * N_IN,
         out_specs=(vmem, vmem),
         scratch_shapes=[
+            *[pltpu.VMEM(a.shape, a.dtype) for a in operands[:-1]],
+            dma((N_IN + 2,)),
             pltpu.VMEM((N_DEV, 16, 128), BF16),
             pltpu.VMEM((N_DEV, 16, 128), BF16),
             pltpu.VMEM((32, 128), BF16),
@@ -378,37 +406,35 @@
             dma((TR, 2, 4)),
         ],
         compiler_params=pltpu.CompilerParams(
-            collective_id=0, has_side_effects=True, vmem_limit_bytes=56 << 20
+            collective_id=0, has_side_effects=True, vmem_limit_bytes=28 << 20
         ),
-    )(*operands)
-
-
-def update_kernel(ranks, trail, products, neg_v, out):
-    i = pl.program_id(0)
-    half = pl.program_id(1)
-    for j in range(2):
-        rank = ranks[i, half * 2 + j]
-        left = jnp.where(iota((K, B), 0) < rank, trail[0, j, 0], jnp.zeros((), BF16))
-        rows = pl.ds(K * j, K)
-        lhs = jnp.concatenate([left, products[0, rows]], axis=0)
-        rhs = jnp.concatenate([trail[0, j, 1], neg_v[rows]], axis=0)
-        out[0, j] = dot(lhs, rhs, TN).astype(BF16)
-
-
-def update(ranks, trail, products, neg_v):
+    )(near_count, *[pltpu.with_memory_space_constraint(a, pltpu.HBM) for a in operands])
+
+
+def update_kernel(lefts, rights, out, made, sems):
+    copies = []
+    for i in range(TR):
+        for j in range(TC):
+            made[i, j] = dot(lefts[i, j], rights[i, j], TN).astype(BF16)
+            copies.append(pltpu.make_async_copy(made.at[i, j], out.at[i, j], sems.at[i, j]))
+            copies[-1].start()
+    for copy in copies:
+        copy.wait()
+
+
+def update(lefts, rights):
+    vmem = pl.BlockSpec(memory_space=pltpu.VMEM)
     return pl.pallas_call(
         update_kernel,
-        grid=(TR, 2),
         out_shape=jax.ShapeDtypeStruct((TR, TC, B, B), BF16),
-        in_specs=[
-            pl.BlockSpec(memory_space=pltpu.SMEM),
-            pl.BlockSpec((1, 2, 2, K, B), lambda i, h: (i, h, 0, 0, 0)),
-            pl.BlockSpec((1, 2 * K, B), lambda i, h: (i, h, 0)),
-            pl.BlockSpec((2 * K, B), lambda i, h: (h, 0)),
+        in_specs=[vmem, vmem],
+        out_specs=pl.BlockSpec(memory_space=pltpu.HBM),
+        scratch_shapes=[
+            pltpu.VMEM((TR, TC, B, B), BF16),
+            pltpu.SemaphoreType.DMA((TR, TC)),
         ],
-        out_specs=pl.BlockSpec((1, 2, B, B), lambda i, h: (i, h, 0, 0)),
-        compiler_params=pltpu.CompilerParams(vmem_limit_bytes=32 << 20),
-    )(ranks, trail, products, neg_v)
+        compiler_params=pltpu.CompilerParams(vmem_limit_bytes=30 << 20),
+    )(lefts, rights)
 
 
 def per_device(
@@ -424,18 +450,20 @@
     near_row,
     near_count,
 ):
-    products, neg_v = exchange(
+    lefts, rights = exchange(
+        near_count,
+        near_dest.reshape(1, NEAR),
+        near_row.reshape(1, NEAR),
         near_vals,
-        near_dest,
-        near_row.reshape(1, NEAR),
-        near_count,
+        diag_tile,
+        panel_row,
+        pivot_order.reshape(1, B),
+        pattern.reshape(1, TC),
         panel_col,
-        diag_tile,
-        pivot_order.reshape(1, B),
-        panel_row,
-        pattern,
-    )
-    return update(tile_ranks, trail_factors, products, neg_v)
+        tile_ranks.T,
+        trail_factors,
+    )
+    return update(lefts, rights)
 
 
 def solution(mesh):

time: 79.3 us -> 59.9 us (0.76)
  Pallas kernels: 71.4 us -> 59.2 us
  local copies, waits for them, and re-layouts: 6.95 us -> 0 us
    pallas_call x2, Pallas kernels: 71.4 us -> 59.2 us  [the longest x1 52.8 us: exchange(): pl.pallas_call(exchange_kernel, out_shape=(jax.ShapeDtypeStruct((TR, TC,...]
    unnamed x8 -> x0, local copies, waits for them, and re-layouts: 6.95 us -> none
where the time goes in v2:
time: 59.9 us; the launch traced here: 59.8 us
  Pallas kernels  59.2 us (99%)
  between operations  0.66 us (1%)
    pallas_call x1, Pallas kernels, exchange(): pl.pallas_call(exchange_kernel, out_shape=(jax.ShapeDtypeStruct((TR, TC,...  52.8 us
    pallas_call x1, Pallas kernels, update(): pl.pallas_call(update_kernel, out_shape=jax.ShapeDtypeStruct((TR, TC, B,...  6.39 us

profile of v2, /device:TPU:0, one launch (start us, length us, event | category | flops | bytes accessed | tf_op | source)
XLA Modules:
  0.0 59.8 jit_solution(3055066124243280551)
XLA Ops:
  0.7 52.8 %shard_map.109 = (bf16[8,4,128,512]{3,2,1,0:T(8,128)(2,1)S(1)}, bf16[8,4,128,512]{3,2,1,0:T(8,128)(2,1)S(1)}) custom-call(s32[1]{0:T(128)S(6)} %copy.12.near_count, s32[1,256]{1,0:T(1,128)} %bitcast.7, s32[1,256]{1,0:T(1,128)} %bitcast.8, bf16[256,512]{1,0:T(8,128)(2,1)} %refs_2_.1, f32[4,512]{1,0:T(4,128)} %refs_3_.1, bf16[4,2,64,64]{3,2,1,0:T(8,128)(2,1)} %refs_4_.1, ...), custom_call_target="tpu_custom_call" | custom-call | tf_op jit(solution)/shard_map/pallas_call | solution.py:383
  53.4 6.4 %shard_map.110 = bf16[8,4,512,512]{3,2,1,0:T(8,128)(2,1)} custom-call(bf16[8,4,128,512]{3,2,1,0:T(8,128)(2,1)S(1)} %get-tuple-element.7.lefts, bf16[8,4,128,512]{3,2,1,0:T(8,128)(2,1)S(1)} %get-tuple-element.8.rights), custom_call_target="tpu_custom_call" | custom-call | tf_op jit(solution)/shard_map/pallas_call | solution.py:427

commit v3 on v2

--- a/solution.py
+++ b/solution.py
@@ -60,6 +60,7 @@
     one_recv,
     ring_send,
     ring_recv,
+    row_ready,
     ) = refs[2 * N_IN + 2 :]
     loads = [
         pltpu.make_async_copy(source, place, local_sems.at[k])
@@ -86,14 +87,13 @@
 
     barrier = pltpu.get_barrier_semaphore()
 
-    def greet(step, carry):
-        other = lax.rem(me + step, N_DEV)
-        pl.semaphore_signal(
-            barrier, inc=1, device_id=(other // N_COL, lax.rem(other, N_COL)), device_id_type=MESH
-        )
-        return carry
-
-    lax.fori_loop(1, N_DEV, greet, 0)
+    row_peers = [(lax.rem(row + k, N_ROW), col) for k in range(1, N_ROW)]
+    col_peers = [(row, lax.rem(col + k, N_COL)) for k in range(1, N_COL)]
+    for peer in col_peers + row_peers:
+        pl.semaphore_signal(barrier, inc=1, device_id=peer, device_id_type=MESH)
+    pl.semaphore_wait(barrier, len(col_peers) + len(row_peers))
+    for peer in col_peers:
+        pl.semaphore_signal(row_ready, inc=1, device_id=peer, device_id_type=MESH)
 
     def copy(src, dst, sems, device):
         return pltpu.make_async_remote_copy(
@@ -142,12 +142,9 @@
         load.wait()
 
     own_rows = diag_tile[...]
-    diag_x[x] = jnp.where(
-        iota((16, B), 0) // 4 == x, jnp.concatenate([own_rows] * 4, axis=0), 0.0
-    )
+    diag_x[x] = own_rows
     panel_all[z, core] = panel_row[...]
 
-    pl.semaphore_wait(barrier, N_DEV - 1)
 
     ones = iter(range(64))
 
@@ -189,8 +186,8 @@
         ).start()
         return carry
 
-    lax.fori_loop(1, N_DEV, send_near, 0)
-    near_in[me_in] = near_out[me]
+    pl.semaphore_wait(row_ready, len(col_peers))
+    lax.fori_loop(1, 65, send_near, 0)
 
     finish(meta_row_copies)
     total = meta_own[...].astype(F32)
@@ -202,12 +199,8 @@
         for k in range(1, N_COL)
     ]
     begin(meta_copies)
-
-    finish(diag_x_copies)
-    mine = diag_all.at[z, core, pl.ds(pl.multiple_of(16 * y, 16), 16)]
-    mine[...] = (diag_x[0] + diag_x[1]) + (diag_x[2] + diag_x[3])
-    diag_y_copies = [copy(mine, mine, sems(), (row, 4 * lax.rem(y + k, 4) + x)) for k in (1, 3, 2)]
-    begin(diag_y_copies)
+    lax.fori_loop(65, N_DEV, send_near, 0)
+    near_in[me_in] = near_out[me]
 
     finish(meta_copies)
     slots = N_DEV * CAP
@@ -219,7 +212,6 @@
     target = jnp.sum(jnp.where(iota((slots, 128), 1) == lane, named, 0.0), axis=1, keepdims=True)
     landing = jnp.where(target.astype(jnp.int32) - 1 == iota((slots, 256), 1), 1.0, 0.0).astype(BF16)
 
-    finish(diag_y_copies)
     near_all = near_in.at[pl.ds(0, N_DEV - 1)]
     pltpu.make_async_copy(near_all, near_all, near_sems[1]).wait()
     both = near_in[...].astype(F32).reshape(64, 2, 16, 128)
@@ -273,6 +265,34 @@
     two = [second_phase(i) for i in range(TR)]
     for i in range(TR):
         begin(one[i][:2])
+    finish(diag_x_copies)
+    mine = diag_all.at[z, core, pl.ds(pl.multiple_of(16 * y, 16), 16)]
+    mine[...] = jnp.concatenate([diag_x[k] for k in range(4)], axis=0)
+    diag_y_copies = [copy(mine, mine, sems(), (row, 4 * lax.rem(y + k, 4) + x)) for k in (1, 3, 2)]
+    begin(diag_y_copies)
+
+    panel_z_copies = [
+        copy(
+            panel_all.at[z, core],
+            panel_all.at[z, core],
+            sems(),
+            (2 * lax.rem(z + k, 4) + core, col),
+        )
+        for k in (1, 3, 2)
+    ]
+    begin(panel_z_copies)
+
+
+    for i in range(TR):
+        one[i][0].wait_recv()
+        begin([one[i][2]])
+        one[i][1].wait_recv()
+        begin([one[i][3]])
+    for i in range(TR):
+        finish(one[i][2:])
+        begin(two[i][:2])
+
+    finish(diag_y_copies)
     diag_z_copies = [
         copy(
             diag_all.at[z, core],
@@ -284,26 +304,6 @@
     ]
     begin(diag_z_copies)
 
-    panel_z_copies = [
-        copy(
-            panel_all.at[z, core],
-            panel_all.at[z, core],
-            sems(),
-            (2 * lax.rem(z + k, 4) + core, col),
-        )
-        for k in (1, 3, 2)
-    ]
-    begin(panel_z_copies)
-
-
-    for i in range(TR):
-        one[i][0].wait_recv()
-        begin([one[i][2]])
-        one[i][1].wait_recv()
-        begin([one[i][3]])
-    for i in range(TR):
-        finish(one[i][2:])
-        begin(two[i][:2])
 
     for i in range(0, 4):
         two[i][0].wait_recv()
@@ -396,7 +396,7 @@
             pltpu.VMEM((32, 128), BF16),
             pltpu.VMEM((8, 32, 128), BF16),
             pltpu.VMEM((16, 32, 128), BF16),
-            pltpu.VMEM((4, 16, B), F32),
+            pltpu.VMEM((4, 4, B), F32),
             pltpu.VMEM((4, 2, 64, B), F32),
             pltpu.VMEM((4, 2, TC, 2, K, 64), BF16),
             pltpu.VMEM((TR, 4, 4, RB, B), BF16),
@@ -404,6 +404,7 @@
             dma((48,)),
             dma((TR, 2, 4)),
             dma((TR, 2, 4)),
+            pltpu.SemaphoreType.REGULAR,
         ],
         compiler_params=pltpu.CompilerParams(
             collective_id=0, has_side_effects=True, vmem_limit_bytes=28 << 20

time: 59.9 us -> 57.8 us (0.965)
  Pallas kernels: 59.2 us -> 57.1 us
    pallas_call x1, Pallas kernels: 52.8 us -> 50.7 us  [exchange(): pl.pallas_call(exchange_kernel, out_shape=(jax.ShapeDtypeStruct((TR, TC,...]
where the time goes in v3:
time: 57.8 us; the launch traced here: 57.7 us
  Pallas kernels  57.1 us (99%)
  between operations  0.66 us (1%)
    pallas_call x1, Pallas kernels, exchange(): pl.pallas_call(exchange_kernel, out_shape=(jax.ShapeDtypeStruct((TR, TC,...  50.7 us
    pallas_call x1, Pallas kernels, update(): pl.pallas_call(update_kernel, out_shape=jax.ShapeDtypeStruct((TR, TC, B,...  6.4 us

profile of v3, /device:TPU:0, one launch (start us, length us, event | category | flops | bytes accessed | tf_op | source)
XLA Modules:
  0.0 57.7 jit_solution(8850164806927170953)
XLA Ops:
  0.7 50.7 %shard_map.109 = (bf16[8,4,128,512]{3,2,1,0:T(8,128)(2,1)S(1)}, bf16[8,4,128,512]{3,2,1,0:T(8,128)(2,1)S(1)}) custom-call(s32[1]{0:T(128)S(6)} %copy.12.near_count, s32[1,256]{1,0:T(1,128)} %bitcast.7, s32[1,256]{1,0:T(1,128)} %bitcast.8, bf16[256,512]{1,0:T(8,128)(2,1)} %refs_2_.1, f32[4,512]{1,0:T(4,128)} %refs_3_.1, bf16[4,2,64,64]{3,2,1,0:T(8,128)(2,1)} %refs_4_.1, ...), custom_call_target="tpu_custom_call" | custom-call | tf_op jit(solution)/shard_map/pallas_call | solution.py:383
  51.3 6.4 %shard_map.110 = bf16[8,4,512,512]{3,2,1,0:T(8,128)(2,1)} custom-call(bf16[8,4,128,512]{3,2,1,0:T(8,128)(2,1)S(1)} %get-tuple-element.7.lefts, bf16[8,4,128,512]{3,2,1,0:T(8,128)(2,1)S(1)} %get-tuple-element.8.rights), custom_call_target="tpu_custom_call" | custom-call | tf_op jit(solution)/shard_map/pallas_call | solution.py:428

commit v4 on v3

--- a/solution.py
+++ b/solution.py
@@ -92,7 +92,7 @@
     for peer in col_peers + row_peers:
         pl.semaphore_signal(barrier, inc=1, device_id=peer, device_id_type=MESH)
     pl.semaphore_wait(barrier, len(col_peers) + len(row_peers))
-    for peer in col_peers:
+    for peer in row_peers:
         pl.semaphore_signal(row_ready, inc=1, device_id=peer, device_id_type=MESH)
 
     def copy(src, dst, sems, device):
@@ -176,18 +176,30 @@
 
     near_sems = sems()
 
-    def send_near(step, carry):
-        other = lax.rem(me + step, N_DEV)
-        copy(
-            near_out.at[other],
-            near_in.at[me_in],
-            near_sems,
-            (other // N_COL, lax.rem(other, N_COL)),
-        ).start()
-        return carry
-
-    pl.semaphore_wait(row_ready, len(col_peers))
-    lax.fori_loop(1, 65, send_near, 0)
+    def send_near(target_row, target_col):
+        other = target_row * N_COL + target_col
+        copy(near_out.at[other], near_in.at[me_in], near_sems, (target_row, target_col)).start()
+
+    offsets = [
+        (dz, dcore, dy, dx)
+        for dz in range(4)
+        for dcore in range(2)
+        for dy in range(4)
+        for dx in range(4)
+        if (dz, dcore) != (0, 0) or (dy, dx) != (0, 0)
+    ]
+    hops = [0, 1, 2, 1]
+    offsets.sort(key=lambda o: (-hops[o[0]] - hops[o[2]] - hops[o[3]], (7 * o[0] + 5 * o[2] + 3 * o[3] + o[1]) % 8))
+
+    def send_far(some):
+        for dz, dcore, dy, dx in some:
+            other_core = lax.rem(core + dcore, 2)
+            send_near(
+                2 * lax.rem(z + dz, 4) + other_core, 4 * lax.rem(y + dy, 4) + lax.rem(x + dx, 4)
+            )
+
+    pl.semaphore_wait(row_ready, len(row_peers))
+    send_far(offsets[:80])
 
     finish(meta_row_copies)
     total = meta_own[...].astype(F32)
@@ -199,8 +211,15 @@
         for k in range(1, N_COL)
     ]
     begin(meta_copies)
-    lax.fori_loop(65, N_DEV, send_near, 0)
+    send_far(offsets[80:])
     near_in[me_in] = near_out[me]
+
+    finish(diag_x_copies)
+    mine = diag_all.at[z, core, pl.ds(pl.multiple_of(16 * y, 16), 16)]
+    mine[...] = jnp.concatenate([diag_x[k] for k in range(4)], axis=0)
+    diag_y_copies = [copy(mine, mine, sems(), (row, 4 * lax.rem(y + k, 4) + x)) for k in (1, 3, 2)]
+    begin(diag_y_copies)
+
 
     finish(meta_copies)
     slots = N_DEV * CAP
@@ -265,12 +284,6 @@
     two = [second_phase(i) for i in range(TR)]
     for i in range(TR):
         begin(one[i][:2])
-    finish(diag_x_copies)
-    mine = diag_all.at[z, core, pl.ds(pl.multiple_of(16 * y, 16), 16)]
-    mine[...] = jnp.concatenate([diag_x[k] for k in range(4)], axis=0)
-    diag_y_copies = [copy(mine, mine, sems(), (row, 4 * lax.rem(y + k, 4) + x)) for k in (1, 3, 2)]
-    begin(diag_y_copies)
-
     panel_z_copies = [
         copy(
             panel_all.at[z, core],
@@ -288,10 +301,6 @@
         begin([one[i][2]])
         one[i][1].wait_recv()
         begin([one[i][3]])
-    for i in range(TR):
-        finish(one[i][2:])
-        begin(two[i][:2])
-
     finish(diag_y_copies)
     diag_z_copies = [
         copy(
@@ -304,6 +313,10 @@
     ]
     begin(diag_z_copies)
 
+
+    for i in range(TR):
+        finish(one[i][2:])
+        begin(two[i][:2])
 
     for i in range(0, 4):
         two[i][0].wait_recv()
@@ -322,12 +335,11 @@
     pivot_col = jnp.sum(jnp.where(wide_eye, pivot_order[...], 0), axis=1, keepdims=True)
     pivoting = jnp.where(pivot_col == iota((B, B), 1), 1.0, 0.0).astype(BF16)
 
-    for i in range(4, 8):
+    for i in range(4, 6):
         two[i][0].wait_recv()
         begin([two[i][2]])
         two[i][1].wait_recv()
         begin([two[i][3]])
-
     finish(core_copies)
     tile = diag_all[...].reshape(B, B)
     high, low_part = split(tile)
@@ -356,6 +368,12 @@
 
     inner = once(lead)
     images = (2.0 * inner - once(through_pivot(inner))).astype(BF16)
+
+    for i in range(6, 8):
+        two[i][0].wait_recv()
+        begin([two[i][2]])
+        two[i][1].wait_recv()
+        begin([two[i][3]])
 
     for load in loads[9:]:
         load.wait()

time: 57.8 us -> 55.9 us (0.967)
  Pallas kernels: 57.1 us -> 55.2 us
    pallas_call x1, Pallas kernels: 50.7 us -> 48.8 us  [exchange(): pl.pallas_call(exchange_kernel, out_shape=(jax.ShapeDtypeStruct((TR, TC,...]
where the time goes in v4:
time: 55.9 us; the launch traced here: 55.8 us
  Pallas kernels  55.2 us (99%)
  between operations  0.66 us (1%)
    pallas_call x1, Pallas kernels, exchange(): pl.pallas_call(exchange_kernel, out_shape=(jax.ShapeDtypeStruct((TR, TC,...  48.8 us
    pallas_call x1, Pallas kernels, update(): pl.pallas_call(update_kernel, out_shape=jax.ShapeDtypeStruct((TR, TC, B,...  6.4 us

profile of v4, /device:TPU:0, one launch (start us, length us, event | category | flops | bytes accessed | tf_op | source)
XLA Modules:
  0.0 55.8 jit_solution(8535366004989497338)
XLA Ops:
  0.7 48.8 %shard_map.109 = (bf16[8,4,128,512]{3,2,1,0:T(8,128)(2,1)S(1)}, bf16[8,4,128,512]{3,2,1,0:T(8,128)(2,1)S(1)}) custom-call(s32[1]{0:T(128)S(6)} %copy.12.near_count, s32[1,256]{1,0:T(1,128)} %bitcast.7, s32[1,256]{1,0:T(1,128)} %bitcast.8, bf16[256,512]{1,0:T(8,128)(2,1)} %refs_2_.1, f32[4,512]{1,0:T(4,128)} %refs_3_.1, bf16[4,2,64,64]{3,2,1,0:T(8,128)(2,1)} %refs_4_.1, ...), custom_call_target="tpu_custom_call" | custom-call | tf_op jit(solution)/shard_map/pallas_call | solution.py:401
  49.4 6.4 %shard_map.110 = bf16[8,4,512,512]{3,2,1,0:T(8,128)(2,1)} custom-call(bf16[8,4,128,512]{3,2,1,0:T(8,128)(2,1)S(1)} %get-tuple-element.7.lefts, bf16[8,4,128,512]{3,2,1,0:T(8,128)(2,1)S(1)} %get-tuple-element.8.rights), custom_call_target="tpu_custom_call" | custom-call | tf_op jit(solution)/shard_map/pallas_call | solution.py:446

commit v5 on v4

--- a/solution.py
+++ b/solution.py
@@ -186,7 +186,7 @@
         for dcore in range(2)
         for dy in range(4)
         for dx in range(4)
-        if (dz, dcore) != (0, 0) or (dy, dx) != (0, 0)
+        if (dz, dcore) != (0, 0) and (dy, dx) != (0, 0)
     ]
     hops = [0, 1, 2, 1]
     offsets.sort(key=lambda o: (-hops[o[0]] - hops[o[2]] - hops[o[3]], (7 * o[0] + 5 * o[2] + 3 * o[3] + o[1]) % 8))
@@ -198,8 +198,10 @@
                 2 * lax.rem(z + dz, 4) + other_core, 4 * lax.rem(y + dy, 4) + lax.rem(x + dx, 4)
             )
 
+    for peer in col_peers + row_peers:
+        send_near(*peer)
     pl.semaphore_wait(row_ready, len(row_peers))
-    send_far(offsets[:80])
+    send_far(offsets[:60])
 
     finish(meta_row_copies)
     total = meta_own[...].astype(F32)
@@ -211,7 +213,7 @@
         for k in range(1, N_COL)
     ]
     begin(meta_copies)
-    send_far(offsets[80:])
+    send_far(offsets[60:])
     near_in[me_in] = near_out[me]
 
     finish(diag_x_copies)
@@ -243,8 +245,6 @@
     arrived = jnp.concatenate(columns, axis=1).astype(BF16)
     additions = dot(landing, arrived, TN)
     corrected = (panel_col[...].astype(F32) + additions.reshape(TR, RB, B)).astype(BF16)
-    for i in range(TR):
-        grid[i, y, x] = corrected[i]
 
     def ring_copy(i, phase, k, part, device):
         return copy(part, part, (ring_send.at[i, phase, k], ring_recv.at[i, phase, k]), device)
@@ -283,6 +283,7 @@
     one = [first_phase(i) for i in range(TR)]
     two = [second_phase(i) for i in range(TR)]
     for i in range(TR):
+        grid[i, y, x] = corrected[i]
         begin(one[i][:2])
     panel_z_copies = [
         copy(
@@ -383,15 +384,21 @@
             lefts[i, j, 0:K] = jnp.where(kept, lefts[i, j, 0:K], jnp.zeros((), BF16))
             rights[i, j, K : 2 * K] = neg_v[K * j : K * j + K]
 
+    late = [c for copies in two for c in copies]
+    for c in started:
+        if not any(c is other for other in late):
+            c.wait_send()
+    pltpu.make_async_copy(near_all, near_all, near_sems[0]).wait()
+
     for i in range(TR):
+        for c in two[i][:2]:
+            c.wait_send()
         finish(two[i][2:])
         product = dot(images, grid[i].reshape(B, B), NT).astype(BF16)
         for j in range(TC):
             lefts[i, j, K : 2 * K] = product[K * j : K * j + K]
-
-    for c in started:
-        c.wait_send()
-    pltpu.make_async_copy(near_all, near_all, near_sems[0]).wait()
+        for c in two[i][2:]:
+            c.wait_send()
 
 
 def exchange(near_count, *operands):

time: 55.9 us -> 55.6 us (level)
  no operation moved by 1% of the time
where the time goes in v5:
time: 55.6 us; the launch traced here: 55.5 us
  Pallas kernels  54.8 us (99%)
  between operations  0.66 us (1%)
    pallas_call x1, Pallas kernels, exchange(): pl.pallas_call(exchange_kernel, out_shape=(jax.ShapeDtypeStruct((TR, TC,...  48.4 us
    pallas_call x1, Pallas kernels, update(): pl.pallas_call(update_kernel, out_shape=jax.ShapeDtypeStruct((TR, TC, B,...  6.39 us

profile of v5, /device:TPU:0, one launch (start us, length us, event | category | flops | bytes accessed | tf_op | source)
XLA Modules:
  0.0 55.5 jit_solution(13699338871053816942)
XLA Ops:
  0.7 48.4 %shard_map.109 = (bf16[8,4,128,512]{3,2,1,0:T(8,128)(2,1)S(1)}, bf16[8,4,128,512]{3,2,1,0:T(8,128)(2,1)S(1)}) custom-call(s32[1]{0:T(128)S(6)} %copy.12.near_count, s32[1,256]{1,0:T(1,128)} %bitcast.7, s32[1,256]{1,0:T(1,128)} %bitcast.8, bf16[256,512]{1,0:T(8,128)(2,1)} %refs_2_.1, f32[4,512]{1,0:T(4,128)} %refs_3_.1, bf16[4,2,64,64]{3,2,1,0:T(8,128)(2,1)} %refs_4_.1, ...), custom_call_target="tpu_custom_call" | custom-call | tf_op jit(solution)/shard_map/pallas_call | solution.py:408
  49.1 6.4 %shard_map.110 = bf16[8,4,512,512]{3,2,1,0:T(8,128)(2,1)} custom-call(bf16[8,4,128,512]{3,2,1,0:T(8,128)(2,1)S(1)} %get-tuple-element.7.lefts, bf16[8,4,128,512]{3,2,1,0:T(8,128)(2,1)S(1)} %get-tuple-element.8.rights), custom_call_target="tpu_custom_call" | custom-call | tf_op jit(solution)/shard_map/pallas_call | solution.py:453
